TPU v7x, 32 devices: a whole 2x2x4 slice. The times are simulated.
32 devices in a mesh: section: 4 (over y, x), seq: 2 (over core), tensor: 4 (over z).
Axes of the slice: x: 2, y: 2, z: 4, core: 2. Of those that a mesh axis runs over, the one named last changes fastest.
Arguments:
- inputs: bfloat16 [2, 256, 2, 768], P(None, ('seq', 'tensor')), may hold values from -6 to 6
- cotangent: bfloat16 [2, 256, 2, 768], P(None, ('seq', 'tensor')), may hold values from -6 to 6
- lengths: int32 [2, 2], replicated, may hold values from 64 to 256, as said below
- chosen: int32 [4, 2, 2, 12, 4, 64], P('section', None, None, 'tensor', 'seq'), may hold values from 0 to 128, as said below
- ln1_gain: float32 [4, 768], P('section'), may hold values from 0.5 to 1.5
- ln1_shift: float32 [4, 768], P('section'), may hold values from -1.5 to 1.5
- w_qkv: bfloat16 [4, 3, 768, 768], P('section', None, None, 'tensor'), may hold values from -0.21875 to 0.21875
- b_qv: float32 [4, 2, 768], P('section', None, 'tensor'), may hold values from -1.5 to 1.5
- w_out: bfloat16 [4, 768, 768], P('section', 'tensor'), may hold values from -0.625 to 0.625
- b_out: float32 [4, 768], P('section'), may hold values from -1.5 to 1.5
- ln2_gain: float32 [4, 768], P('section'), may hold values from 0.5 to 1.5
- ln2_shift: float32 [4, 768], P('section'), may hold values from -1.5 to 1.5
- w_fc: bfloat16 [4, 768, 3072], P('section', None, 'tensor'), may hold values from -0.21875 to 0.21875
- b_fc: float32 [4, 3072], P('section', 'tensor'), may hold values from -1.5 to 1.5
- w_proj: bfloat16 [4, 3072, 768], P('section', 'tensor'), may hold values from -0.109375 to 0.109375
- b_proj: float32 [4, 768], P('section'), may hold values from -1.5 to 1.5
Outputs:
- activations: bfloat16 [4, 2, 256, 2, 768], P('section', None, ('seq', 'tensor'))
- in_grads: bfloat16 [4, 2, 256, 2, 768], P('section', None, ('seq', 'tensor'))
- grad_ln1_gain: float32 [4, 768], P('section')
- grad_ln1_shift: float32 [4, 768], P('section')
- grad_w_qkv: float32 [4, 3, 768, 768], P('section', None, 'seq', 'tensor')
- grad_b_qv: float32 [4, 2, 768], P('section')
- grad_w_out: float32 [4, 768, 768], P('section', 'tensor', 'seq')
- grad_b_out: float32 [4, 768], P('section')
- grad_ln2_gain: float32 [4, 768], P('section')
- grad_ln2_shift: float32 [4, 768], P('section')
- grad_w_fc: float32 [4, 768, 3072], P('section', 'seq', 'tensor')
- grad_b_fc: float32 [4, 3072], P('section')
- grad_w_proj: float32 [4, 3072, 768], P('section', 'tensor', 'seq')
- grad_b_proj: float32 [4, 768], P('section')
Inputs may be any that keep to these rules, and one draw needn't show every extreme that they name: `lengths`: in each micro-batch one sequence, drawn from the seed, is full (256 positions). `chosen`: entries of query block b are positions of the same sequence; where b * 64 >= 64 they lie in 0 to b * 64 - 64 and the last entry of each block and head equals b * 64 - 64; in earlier blocks every entry is 0.
All inputs are finite; a program needn't handle non-finite values.
Results may differ from a plain program's by a relative error of at most 0.025.
Values may be sent and summed in bfloat16 or wider, within the bound.
A program may use at most 192 MiB of HBM per device.

v0:
```python
import functools
import types

import jax
import jax.numpy as jnp
from jax import lax
from jax.experimental import pallas as pl
from jax.experimental.pallas import tpu as pltpu
from jax.sharding import PartitionSpec as P

HDIM = 64
WIN = 64
QB = 64
KSEL = 64


NORM_EPS = 1e-05
MASKED = -1000000000.0


def from_behind(value, axis, steps):
    count = lax.axis_size(axis)
    first, last = (max(0, -steps), min(count, count - steps))
    return lax.ppermute(value, axis, [(source, source + steps) for source in range(first, last)])


def layer_norm(values, gain, shift):
    average = jnp.mean(values, axis=-1, keepdims=True)
    centred = values - average
    variance = jnp.mean(centred * centred, axis=-1, keepdims=True)
    return centred * lax.rsqrt(variance + NORM_EPS) * gain + shift


def gelu_tanh(values):
    return (
        0.5
        * values
        * (1.0 + jnp.tanh(0.7978845608028654 * (values + 0.044715 * values * values * values)))
    )


def gather_rows(row_block):
    return lax.all_gather(row_block, "tensor", axis=0, tiled=True)


def scatter_product(left_rows, weight, formula):
    return lax.psum_scatter(
        jnp.einsum(formula, left_rows, weight, preferred_element_type=jnp.float32).astype(
            jnp.bfloat16
        ),
        "tensor",
        scatter_dimension=0,
        tiled=True,
    ).astype(jnp.float32)


def near_slabs(full_rows, seq_start, seq_first, length_local):
    buckets = full_rows.shape[1]
    heads_local = full_rows.shape[2] // HDIM
    blocks = length_local // QB
    earlier = lax.dynamic_slice_in_dim(full_rows, jnp.maximum(seq_start - WIN, 0), WIN, 0)
    earlier = jnp.where(seq_first, jnp.zeros_like(earlier), earlier)
    local_part = lax.dynamic_slice_in_dim(full_rows, seq_start, length_local, 0)
    segment = jnp.concatenate([earlier, local_part], 0).reshape(
        length_local + WIN, buckets, heads_local, HDIM
    )
    return jnp.concatenate(
        [
            segment[offset_index * QB : offset_index * QB + length_local].reshape(
                blocks, QB, buckets, heads_local, HDIM
            )
            for offset_index in range(WIN // QB + 1)
        ],
        1,
    )


def far_rows(full_rows, flat_index):
    total_rows, buckets, feature_width = full_rows.shape
    heads_local = feature_width // HDIM
    return jnp.take(full_rows.reshape(total_rows * buckets * heads_local, HDIM), flat_index, axis=0)


def key_geometry(chosen_now, seq_start, blocks):
    buckets, heads_local = (chosen_now.shape[0], chosen_now.shape[1])
    bucket_ids = lax.broadcasted_iota(jnp.int32, chosen_now.shape, 0)
    head_ids = lax.broadcasted_iota(jnp.int32, chosen_now.shape, 1)
    flat_index = (chosen_now * buckets + bucket_ids) * heads_local + head_ids
    block_start = seq_start + QB * lax.broadcasted_iota(jnp.int32, (blocks, 1, 1), 0)
    query_ids = lax.broadcasted_iota(jnp.int32, (1, QB, 1), 1)
    key_ids = lax.broadcasted_iota(jnp.int32, (1, 1, WIN + QB), 2)
    distance = query_ids + WIN - key_ids
    near_ok = (distance >= 0) & (distance < WIN) & (block_start + key_ids - WIN >= 0)
    far_ok = chosen_now + WIN <= block_start.reshape(1, 1, blocks, 1)
    near_mask = jnp.broadcast_to(
        near_ok[:, None, None], (blocks, buckets, heads_local, QB, WIN + QB)
    )
    far_mask = jnp.broadcast_to(
        jnp.transpose(far_ok, (2, 0, 1, 3))[:, :, :, None, :],
        (blocks, buckets, heads_local, QB, KSEL),
    )
    return (flat_index, jnp.concatenate([near_mask, far_mask], -1))


def attention_setup(queries, key_rows, value_rows, chosen_now, seq_start, seq_first):
    length_local, buckets, feature_width = queries.shape
    heads_local = feature_width // HDIM
    blocks = length_local // QB
    query_blocks = queries.reshape(blocks, QB, buckets, heads_local, HDIM)
    flat_index, key_mask = key_geometry(chosen_now, seq_start, blocks)
    near_keys = near_slabs(key_rows, seq_start, seq_first, length_local)
    near_values = near_slabs(value_rows, seq_start, seq_first, length_local)
    far_keys = far_rows(key_rows, flat_index)
    far_values = far_rows(value_rows, flat_index)
    near_scores = jnp.einsum(
        "bqnhe,btnhe->bnhqt", query_blocks, near_keys, preferred_element_type=jnp.float32
    )
    far_scores = jnp.einsum(
        "bqnhe,nhbke->bnhqk", query_blocks, far_keys, preferred_element_type=jnp.float32
    )
    scores = jnp.where(
        key_mask, HDIM ** (-0.5) * jnp.concatenate([near_scores, far_scores], -1), MASKED
    )
    return (query_blocks, near_keys, near_values, far_keys, far_values, flat_index, scores)


def attend(queries, key_rows, value_rows, chosen_now, seq_start, seq_first):
    query_blocks, near_keys, near_values, far_keys, far_values, flat_index, scores = (
        attention_setup(queries, key_rows, value_rows, chosen_now, seq_start, seq_first)
    )
    span = WIN + QB
    row_top = jnp.max(scores, -1, keepdims=True)
    exp_terms = jnp.exp(scores - row_top)
    row_total = jnp.sum(exp_terms, -1, keepdims=True)
    softmax_low = (exp_terms / row_total).astype(jnp.bfloat16)
    near_part = jnp.einsum(
        "bnhqt,btnhe->bqnhe",
        softmax_low[..., :span],
        near_values,
        preferred_element_type=jnp.float32,
    )
    far_part = jnp.einsum(
        "bnhqk,nhbke->bqnhe",
        softmax_low[..., span:],
        far_values,
        preferred_element_type=jnp.float32,
    )
    return ((near_part + far_part).reshape(queries.shape), row_top + jnp.log(row_total))


def spread_back(near_grad, far_grad, flat_index, seq_start, seq_first, total_rows):
    blocks, span, buckets, heads_local, head_size = near_grad.shape
    length_local = blocks * QB
    feature_width = heads_local * head_size
    segment = jnp.zeros((length_local + WIN, buckets, heads_local, head_size), jnp.float32)
    for offset_index in range(WIN // QB + 1):
        piece = near_grad[:, offset_index * QB : (offset_index + 1) * QB].reshape(
            length_local, buckets, heads_local, head_size
        )
        segment = segment.at[offset_index * QB : offset_index * QB + length_local].add(piece)
    full_rows = jnp.zeros((total_rows * buckets * heads_local, head_size), jnp.float32)
    full_rows = full_rows.at[flat_index.reshape(-1)].add(far_grad.reshape(-1, head_size))
    full_rows = full_rows.reshape(total_rows, buckets, feature_width)
    local_part = segment[WIN:].reshape(length_local, buckets, feature_width)
    earlier = jnp.where(seq_first, 0.0, segment[:WIN].reshape(WIN, buckets, feature_width))
    full_rows = lax.dynamic_update_slice_in_dim(
        full_rows,
        lax.dynamic_slice_in_dim(full_rows, seq_start, length_local, 0) + local_part,
        seq_start,
        0,
    )
    earlier_start = jnp.maximum(seq_start - WIN, 0)
    full_rows = lax.dynamic_update_slice_in_dim(
        full_rows,
        lax.dynamic_slice_in_dim(full_rows, earlier_start, WIN, 0) + earlier,
        earlier_start,
        0,
    )
    return full_rows


def attend_back(
    queries, key_rows, value_rows, chosen_now, seq_start, seq_first, log_total, grad_mixed
):
    query_blocks, near_keys, near_values, far_keys, far_values, flat_index, scores = (
        attention_setup(queries, key_rows, value_rows, chosen_now, seq_start, seq_first)
    )
    span = WIN + QB
    score_scale = HDIM ** (-0.5)
    grad_blocks = grad_mixed.reshape(query_blocks.shape)
    weights_full = jnp.exp(scores - log_total)
    softmax_low = weights_full.astype(jnp.bfloat16)
    grad_near_weights = jnp.einsum(
        "bqnhe,btnhe->bnhqt", grad_blocks, near_values, preferred_element_type=jnp.float32
    )
    grad_far_weights = jnp.einsum(
        "bqnhe,nhbke->bnhqk", grad_blocks, far_values, preferred_element_type=jnp.float32
    )
    grad_weights = jnp.concatenate([grad_near_weights, grad_far_weights], -1)
    row_dot = jnp.sum(weights_full * grad_weights, -1, keepdims=True)
    grad_scores = (weights_full * (grad_weights - row_dot)).astype(jnp.bfloat16)
    grad_near, grad_far = (grad_scores[..., :span], grad_scores[..., span:])
    grad_queries = score_scale * (
        jnp.einsum("bnhqt,btnhe->bqnhe", grad_near, near_keys, preferred_element_type=jnp.float32)
        + jnp.einsum("bnhqk,nhbke->bqnhe", grad_far, far_keys, preferred_element_type=jnp.float32)
    )
    near_key_grad = score_scale * jnp.einsum(
        "bnhqt,bqnhe->btnhe", grad_near, query_blocks, preferred_element_type=jnp.float32
    )
    far_key_grad = score_scale * jnp.einsum(
        "bnhqk,bqnhe->nhbke", grad_far, query_blocks, preferred_element_type=jnp.float32
    )
    near_value_grad = jnp.einsum(
        "bnhqt,bqnhe->btnhe",
        softmax_low[..., :span],
        grad_blocks,
        preferred_element_type=jnp.float32,
    )
    far_value_grad = jnp.einsum(
        "bnhqk,bqnhe->nhbke",
        softmax_low[..., span:],
        grad_blocks,
        preferred_element_type=jnp.float32,
    )
    total_rows = key_rows.shape[0]
    key_grad = spread_back(
        near_key_grad, far_key_grad, flat_index, seq_start, seq_first, total_rows
    )
    value_grad = spread_back(
        near_value_grad, far_value_grad, flat_index, seq_start, seq_first, total_rows
    )
    return (grad_queries.reshape(queries.shape), key_grad, value_grad)


def forward_pass(hidden, params, chosen_now, query_mask, seq_start, seq_first, finish):
    (
        ln1_gain,
        ln1_shift,
        w_qkv,
        b_qv,
        w_out,
        b_out,
        ln2_gain,
        ln2_shift,
        w_fc,
        b_fc,
        w_proj,
        b_proj,
    ) = params
    hidden_wide = hidden.astype(jnp.float32)
    normed_all = gather_rows(layer_norm(hidden_wide, ln1_gain, ln1_shift).astype(jnp.bfloat16))
    projected = jnp.einsum("pnd,jdc->jpnc", normed_all, w_qkv, preferred_element_type=jnp.float32)
    queries = (projected[0] + b_qv[0]).astype(jnp.bfloat16)
    key_rows, value_rows = (
        lax.all_gather(projected[1].astype(jnp.bfloat16), "seq", axis=0, tiled=True),
        lax.all_gather((projected[2] + b_qv[1]).astype(jnp.bfloat16), "seq", axis=0, tiled=True),
    )
    attended, log_total = attend(queries, key_rows, value_rows, chosen_now, seq_start, seq_first)
    mixed_rows = (attended * query_mask[:, :, None]).astype(jnp.bfloat16)
    middle = hidden_wide + scatter_product(mixed_rows, w_out, "pnc,cd->pnd") + b_out
    normed_mlp = gather_rows(layer_norm(middle, ln2_gain, ln2_shift).astype(jnp.bfloat16))
    pre_active = (
        jnp.einsum("pnd,df->pnf", normed_mlp, w_fc, preferred_element_type=jnp.float32) + b_fc
    )
    active = gelu_tanh(pre_active).astype(jnp.bfloat16)
    if not finish:
        return (
            normed_all,
            queries,
            key_rows,
            value_rows,
            log_total,
            mixed_rows,
            middle,
            normed_mlp,
            pre_active,
            active,
        )
    output = (middle + scatter_product(active, w_proj, "pnf,fd->pnd") + b_proj).astype(jnp.bfloat16)
    return (output, (key_rows, value_rows))


def backward_pass(hidden, upstream, params, chosen_now, query_mask, seq_start, seq_first):
    (
        ln1_gain,
        ln1_shift,
        w_qkv,
        b_qv,
        w_out,
        b_out,
        ln2_gain,
        ln2_shift,
        w_fc,
        b_fc,
        w_proj,
        b_proj,
    ) = params
    (
        normed_all,
        queries,
        key_rows,
        value_rows,
        log_total,
        mixed_rows,
        middle,
        normed_mlp,
        pre_active,
        active,
    ) = forward_pass(hidden, params, chosen_now, query_mask, seq_start, seq_first, False)
    upstream_all = gather_rows(upstream)
    grad_w_proj = jnp.einsum(
        "pnf,pnd->fd", active, upstream_all, preferred_element_type=jnp.float32
    )
    grad_b_proj = jnp.sum(upstream.astype(jnp.float32), axis=(0, 1))
    grad_active = jnp.einsum(
        "pnd,fd->pnf", upstream_all, w_proj, preferred_element_type=jnp.float32
    )
    unused_value, gelu_pull = jax.vjp(gelu_tanh, pre_active)
    grad_pre = gelu_pull(grad_active)[0].astype(jnp.bfloat16)
    grad_w_fc = jnp.einsum("pnd,pnf->df", normed_mlp, grad_pre, preferred_element_type=jnp.float32)
    grad_b_fc = jnp.sum(grad_pre.astype(jnp.float32), axis=(0, 1))
    grad_normed_mlp = scatter_product(grad_pre, w_fc, "pnf,df->pnd")
    unused_norm, second_pull = jax.vjp(layer_norm, middle, ln2_gain, ln2_shift)
    grad_mid_norm, grad_ln2_gain, grad_ln2_shift = second_pull(grad_normed_mlp)
    grad_middle = upstream.astype(jnp.float32) + grad_mid_norm
    grad_branch = grad_middle.astype(jnp.bfloat16)
    grad_b_out = jnp.sum(grad_branch.astype(jnp.float32), axis=(0, 1))
    branch_all = gather_rows(grad_branch)
    grad_w_out = jnp.einsum(
        "pnc,pnd->cd", mixed_rows, branch_all, preferred_element_type=jnp.float32
    )
    grad_mixed = jnp.einsum(
        "pnd,cd->pnc", branch_all, w_out, preferred_element_type=jnp.float32
    ).astype(jnp.bfloat16) * query_mask[:, :, None].astype(jnp.bfloat16)
    grad_queries, key_grad_all, value_grad_all = attend_back(
        queries, key_rows, value_rows, chosen_now, seq_start, seq_first, log_total, grad_mixed
    )
    key_grad, value_grad = (
        lax.psum_scatter(
            key_grad_all.astype(jnp.bfloat16), "seq", scatter_dimension=0, tiled=True
        ).astype(jnp.float32),
        lax.psum_scatter(
            value_grad_all.astype(jnp.bfloat16), "seq", scatter_dimension=0, tiled=True
        ).astype(jnp.float32),
    )
    grad_project = jnp.stack(
        [
            grad_queries.astype(jnp.bfloat16),
            key_grad.astype(jnp.bfloat16),
            value_grad.astype(jnp.bfloat16),
        ],
        2,
    )
    grad_w_qkv = jnp.einsum(
        "pnd,pnjc->jdc", normed_all, grad_project, preferred_element_type=jnp.float32
    )
    grad_b_qv = jnp.sum(grad_project[:, :, 0::2].astype(jnp.float32), axis=(0, 1))
    grad_normed = scatter_product(grad_project, w_qkv, "pnjc,jdc->pnd")
    unused_first, first_pull = jax.vjp(layer_norm, hidden.astype(jnp.float32), ln1_gain, ln1_shift)
    grad_in_norm, grad_ln1_gain, grad_ln1_shift = first_pull(grad_normed)
    grad_hidden = (grad_middle + grad_in_norm).astype(jnp.bfloat16)
    block_grads = (
        grad_ln1_gain,
        grad_ln1_shift,
        grad_w_qkv,
        grad_b_qv,
        grad_w_out,
        grad_b_out,
        grad_ln2_gain,
        grad_ln2_shift,
        grad_w_fc,
        grad_b_fc,
        grad_w_proj,
        grad_b_proj,
    )
    return (grad_hidden, block_grads)


def on_device(
    inputs,
    cotangent,
    lengths,
    chosen,
    ln1_gain,
    ln1_shift,
    w_qkv,
    b_qv,
    w_out,
    b_out,
    ln2_gain,
    ln2_shift,
    w_fc,
    b_fc,
    w_proj,
    b_proj,
):
    params = tuple(
        (
            weight_array[0]
            for weight_array in (
                ln1_gain,
                ln1_shift,
                w_qkv,
                b_qv,
                w_out,
                b_out,
                ln2_gain,
                ln2_shift,
                w_fc,
                b_fc,
                w_proj,
                b_proj,
            )
        )
    )
    section_index = lax.axis_index("section")
    section_count = lax.axis_size("section")
    seq_index = lax.axis_index("seq")
    tensor_index = lax.axis_index("tensor")
    tensor_count = lax.axis_size("tensor")
    micro_count, rows_local, buckets, feature_width = inputs.shape
    length_local = rows_local * tensor_count
    heads_width = w_qkv.shape[-1]
    seq_start = seq_index * length_local
    seq_first = seq_index == 0
    positions = seq_start + lax.broadcasted_iota(jnp.int32, (micro_count, length_local, buckets), 1)
    mask_all = (positions < lengths[:, None, :]).astype(jnp.float32)
    mask_rows = lax.dynamic_slice_in_dim(mask_all, tensor_index * rows_local, rows_local, 1)
    step_count = micro_count + section_count - 1
    chosen_section = chosen[0]
    received = jnp.zeros((rows_local, buckets, feature_width), jnp.bfloat16)
    stored = jnp.zeros((micro_count, rows_local, buckets, feature_width), jnp.bfloat16)
    outputs = jnp.zeros_like(stored)
    for step_index in range(step_count):
        micro_index = step_index - section_index
        running = (micro_index >= 0) & (micro_index < micro_count)
        slot_index = jnp.clip(micro_index, 0, micro_count - 1)
        block_in = jnp.where(
            section_index == 0, lax.dynamic_index_in_dim(inputs, slot_index, 0, False), received
        )
        chosen_now = lax.dynamic_index_in_dim(chosen_section, slot_index, 0, False)
        query_mask = lax.dynamic_index_in_dim(mask_all, slot_index, 0, False)
        result, key_pair = forward_pass(
            block_in, params, chosen_now, query_mask, seq_start, seq_first, True
        )
        stored = jnp.where(
            running, lax.dynamic_update_index_in_dim(stored, block_in, slot_index, 0), stored
        )
        outputs = jnp.where(
            running, lax.dynamic_update_index_in_dim(outputs, result, slot_index, 0), outputs
        )
        received = from_behind(result, "section", 1)
    back_received = jnp.zeros((rows_local, buckets, feature_width), jnp.bfloat16)
    in_grads = jnp.zeros_like(stored)
    totals = None
    for step_index in range(step_count):
        micro_index = step_index - (section_count - 1 - section_index)
        running = (micro_index >= 0) & (micro_index < micro_count)
        slot_index = jnp.clip(micro_index, 0, micro_count - 1)
        chosen_now = lax.dynamic_index_in_dim(chosen_section, slot_index, 0, False)
        query_mask = lax.dynamic_index_in_dim(mask_all, slot_index, 0, False)
        local_mask = lax.dynamic_index_in_dim(mask_rows, slot_index, 0, False)
        top_grad = (
            lax.dynamic_index_in_dim(cotangent, slot_index, 0, False).astype(jnp.float32)
            * local_mask[:, :, None]
        ).astype(jnp.bfloat16)
        upstream = jnp.where(section_index == section_count - 1, top_grad, back_received)
        hidden = lax.dynamic_index_in_dim(stored, slot_index, 0, False)
        grad_hidden, block_grads = backward_pass(
            hidden, upstream, params, chosen_now, query_mask, seq_start, seq_first
        )
        block_grads = tuple(
            (jnp.where(running, grad_part, jnp.zeros_like(grad_part)) for grad_part in block_grads)
        )
        totals = (
            block_grads
            if step_index == 0
            else tuple(
                (total_part + grad_part for total_part, grad_part in zip(totals, block_grads))
            )
        )
        in_grads = jnp.where(
            running, lax.dynamic_update_index_in_dim(in_grads, grad_hidden, slot_index, 0), in_grads
        )
        back_received = from_behind(grad_hidden, "section", -1)
    (
        sum_ln1_gain,
        sum_ln1_shift,
        sum_w_qkv,
        sum_b_qv,
        sum_w_out,
        sum_b_out,
        sum_ln2_gain,
        sum_ln2_shift,
        sum_w_fc,
        sum_b_fc,
        sum_w_proj,
        sum_b_proj,
    ) = totals
    part_qkv, part_out, part_fc, part_proj = (
        lax.psum_scatter(
            sum_w_qkv.astype(jnp.bfloat16), "seq", scatter_dimension=1, tiled=True
        ).astype(jnp.float32),
        lax.psum_scatter(
            sum_w_out.astype(jnp.bfloat16), "seq", scatter_dimension=1, tiled=True
        ).astype(jnp.float32),
        lax.psum_scatter(
            sum_w_fc.astype(jnp.bfloat16), "seq", scatter_dimension=0, tiled=True
        ).astype(jnp.float32),
        lax.psum_scatter(
            sum_w_proj.astype(jnp.bfloat16), "seq", scatter_dimension=1, tiled=True
        ).astype(jnp.float32),
    )
    bias_qv = lax.dynamic_update_slice_in_dim(
        jnp.zeros((2, feature_width), jnp.float32), sum_b_qv, tensor_index * heads_width, 1
    )
    units_local = sum_b_fc.shape[0]
    bias_fc = lax.dynamic_update_slice_in_dim(
        jnp.zeros((units_local * tensor_count,), jnp.float32),
        sum_b_fc,
        tensor_index * units_local,
        0,
    )
    small_sums = lax.psum(
        (
            sum_ln1_gain,
            sum_ln1_shift,
            bias_qv,
            sum_b_out,
            sum_ln2_gain,
            sum_ln2_shift,
            bias_fc,
            sum_b_proj,
        ),
        ("seq", "tensor"),
    )
    return (
        outputs[None],
        in_grads[None],
        small_sums[0][None],
        small_sums[1][None],
        part_qkv[None],
        small_sums[2][None],
        part_out[None],
        small_sums[3][None],
        small_sums[4][None],
        small_sums[5][None],
        part_fc[None],
        small_sums[6][None],
        part_proj[None],
        small_sums[7][None],
    )


STREAMS = 2
NRM, NMLP, UPS, BRN, ACT, GPRE, MIX, DQKV = range(8)
F32 = jnp.float32
LOW = jnp.bfloat16
MESH_ID = pl.DeviceIdType.MESH


def dot_nn(left, right):
    return lax.dot_general(left, right, (((1,), (0,)), ((), ())), preferred_element_type=F32)


def dot_nt(left, right):
    return lax.dot_general(left, right, (((1,), (1,)), ((), ())), preferred_element_type=F32)


def dot_tn(left, right):
    return lax.dot_general(left, right, (((0,), (0,)), ((), ())), preferred_element_type=F32)


def standard(rows):
    centred = rows - jnp.mean(rows, axis=-1, keepdims=True)
    scale = lax.rsqrt(jnp.mean(centred * centred, axis=-1, keepdims=True) + NORM_EPS)
    return centred * scale, scale


def standard_back(grad, xhat, scale):
    inner = jnp.mean(grad * xhat, axis=-1, keepdims=True)
    return scale * (grad - jnp.mean(grad, axis=-1, keepdims=True) - xhat * inner)


def column_sum(rows):
    return jnp.sum(rows.astype(F32), axis=0, keepdims=True)


def relay_kernel(names, *refs):
    r = types.SimpleNamespace(**dict(zip(names, refs)))
    a, c, t = (lax.axis_index(name) for name in ("section", "seq", "tensor"))
    lines = lax.axis_size("section")
    chips = lax.axis_size("tensor")
    rows, buckets, width = r.inputs.shape[1:]
    half_width = width // 2
    local = rows * chips
    total = 2 * local
    stream_rows = local // STREAMS
    head_width = r.wo_in.shape[0]
    heads = head_width // HDIM
    blocks = local // QB
    units = r.wp_in.shape[0]
    scale = HDIM ** (-0.5)
    streams = range(STREAMS)

    def remote(src, dst, send, recv, **target):
        return pltpu.make_async_remote_copy(
            src_ref=src,
            dst_ref=dst,
            send_sem=send,
            recv_sem=recv,
            device_id=target,
            device_id_type=MESH_ID,
        )

    def drain(ref, sem):
        pltpu.make_async_copy(ref, ref, sem).wait()

    def row_block(index, size):
        return pl.ds(pl.multiple_of(index * size, size), size)

    near_chip = t + 1 - 2 * (t % 2)
    over_chip = (t + 2) % 4
    across_chip = 3 - t
    middle_chip = (t == 1) | (t == 2)
    end_chip = (t == 0) | (t == 3)
    owned = stream_rows // 2
    mine = row_block(t - 1, owned)
    my_half = row_block(c, local)

    r.kv[...] = jnp.zeros(r.kv.shape, LOW)

    barrier = pltpu.get_barrier_semaphore()
    greeted = 0
    for line in range(lines):
        for chip in range(chips):
            for core in range(2):
                if (line, chip, core) != (0, 0, 0) and (core == 0 or line * chip == 0):
                    there = {
                        "section": (a + line) % lines,
                        "seq": (c + core) % 2,
                        "tensor": (t + chip) % chips,
                    }
                    pl.semaphore_signal(barrier, inc=1, device_id=there, device_id_type=MESH_ID)
                    greeted += 1
    pl.semaphore_wait(barrier, greeted)

    def beside(s):
        return s + 1 - 2 * (s % 2)

    def above(s):
        return (s + 2) % 4

    def store(p):
        return (r.wq, r.wo, r.wf, r.wp)[p]

    def source(p):
        return (r.wq_in, r.wo_in, r.wf_in, r.wp_in)[p]

    def height(p):
        return source(p).shape[0]

    def core_half(p, s, core):
        return store(p).at[s, row_block(core, height(p) // 2)]

    def first_hop(p, s, neighbour, which):
        return remote(
            source(p).at[row_block(c, height(p) // 2)],
            core_half(p, s, c),
            r.w_first_s.at[p, which],
            r.w_first_r.at[s, p],
            section=neighbour,
        )

    def second_hop(p, s, which):
        view = store(p).at[s, row_block(2 * c + which, height(p) // 4)]
        return remote(
            view, view, r.w_second_s.at[s, p], r.w_second_r.at[s, p, which], section=3 - s
        )

    def core_hop(p, s, core):
        view = core_half(p, s, core)
        return remote(view, view, r.w_core_s.at[s, p], r.w_core_r.at[s, p], seq=1 - c)

    def own_copy(p):
        return pltpu.make_async_copy(source(p), store(p).at[a], r.w_own.at[p])

    def pass_on(s, p, which):
        line = (beside(s), above(s))[which]

        @pl.when(a == line)
        def _():
            first_hop(p, s, line, which).wait_recv()
            second_hop(p, s, which).start()
            core_hop(p, s, c).start()

    def pass_all(s, pieces):
        for p in pieces:
            for which in range(2):
                pass_on(s, p, which)

    def pass_far(s, p):
        @pl.when(a == 3 - s)
        def _():
            second_hop(p, s, 0).wait_recv()
            second_hop(p, s, 1).wait_recv()
            core_hop(p, s, c).start()

    def need(s, p):
        @pl.when(s == 0)
        def _():
            if p < 2:
                pass_all(0, (p,))
            pass_far(0, p)

        @pl.when(a == s)
        def _():
            own_copy(p).wait()

        @pl.when(a != s)
        def _():
            core_hop(p, s, 1 - c).wait_recv()

    def small_copy(step, line, slot):
        return remote(
            r.small_own, r.small.at[slot], r.small_s.at[step], r.small_r.at[slot], section=line
        )

    def count_copy(step, line, slot):
        return remote(
            r.count_own.at[line],
            r.count.at[slot],
            r.count_s.at[step],
            r.count_r.at[slot],
            section=line,
        )

    singles = (r.ln1_gain, r.ln1_shift, r.ln2_gain, r.ln2_shift, r.b_out, r.b_proj)
    for place, single in enumerate(singles):
        r.small_own[place : place + 1] = single[...]
    r.small_own[6:7, :units] = r.b_fc[...]
    r.small_own[7:8, :head_width] = r.b_qv[0:1]
    r.small_own[7:8, half_width : half_width + head_width] = r.b_qv[1:2]
    for step in range(1, lines):
        small_copy(step - 1, (a + step) % lines, a).start()
    for p in range(4):
        for which, line in enumerate((beside(a), above(a))):
            first_hop(p, a, line, which).start()
    for p in range(4):
        own_copy(p).start()
    r.small[a] = r.small_own[...]

    def iota(shape, dimension):
        return lax.broadcasted_iota(jnp.int32, shape, dimension)

    square = jnp.where(iota((KSEL, KSEL), 0) == iota((KSEL, KSEL), 1), 1.0, 0.0).astype(LOW)
    position = iota((KSEL, total), 1).astype(F32)
    for pair in range(lines * heads):
        line, head = pair // heads, pair % heads
        columns = dot_nt(square, r.chosen[pair].astype(F32).astype(LOW))
        for block in range(blocks):
            pick = head * blocks + block
            r.count_own[line, pick : pick + 1, :] = jnp.sum(
                jnp.where(columns[:, block : block + 1] == position, 1.0, 0.0),
                axis=0,
                keepdims=True,
            )
    for step in range(1, lines):
        count_copy(step - 1, (a + step) % lines, a).start()
    r.count[a] = r.count_own[a]

    NEAR, OVER, ACROSS = range(3)

    def gather(buffer, s, kind, j, owner, target, slot):
        view = buffer.at[s, j, row_block(owner - 1, owned)]
        return remote(
            view, view, r.ag_s.at[kind, j, slot], r.ag_r.at[kind, j, slot], tensor=target
        )

    def used_before(s, kind):
        return s > 0 if kind < 2 else s < lines - 1

    def gather_start(buffer, s, kind, j):
        @pl.when(used_before(s, kind))
        def _():
            gather_sent(buffer, s, kind, j)

        gather(buffer, s, kind, j, t, over_chip, OVER).start()
        gather(buffer, s, kind, j, t, across_chip, ACROSS).start()
        gather(buffer, s, kind, j, t, near_chip, NEAR).start()

    def gather_wait(buffer, s, kind, j):
        @pl.when(middle_chip)
        def _():
            gather(buffer, s, kind, j, across_chip, across_chip, ACROSS).wait_recv()

        @pl.when(end_chip)
        def _():
            gather(buffer, s, kind, j, near_chip, near_chip, NEAR).wait_recv()
            gather(buffer, s, kind, j, over_chip, over_chip, OVER).wait_recv()

    def gather_sent(buffer, s, kind, j):
        gather(buffer, s, kind, j, t, over_chip, OVER).wait_send()
        gather(buffer, s, kind, j, t, across_chip, ACROSS).wait_send()
        gather(buffer, s, kind, j, t, near_chip, NEAR).wait_send()

    def scatter(s, kind, j, owner, slot):
        return remote(
            r.part.at[kind, j, row_block(owner - 1, owned)],
            r.arrived.at[s, kind, j, slot],
            r.rs_s.at[kind, j, slot],
            r.rs_r.at[kind, j, slot],
            tensor=owner,
        )

    def scatter_start(s, kind, j, product):
        @pl.when(used_before(s, kind))
        def _():
            scatter_sent(s, kind, j)

        r.part[kind, j] = product.astype(LOW)

        @pl.when(end_chip)
        def _():
            scatter(s, kind, j, over_chip, OVER).start()
            scatter(s, kind, j, near_chip, NEAR).start()

        @pl.when(middle_chip)
        def _():
            scatter(s, kind, j, across_chip, ACROSS).start()

    def scatter_sum(s, kind, j):
        result = r.part[kind, j, mine].astype(F32)
        for slot in (NEAR, ACROSS, OVER):
            scatter(s, kind, j, t, slot).wait_recv()
            result = result + r.arrived[s, kind, j, slot].astype(F32)
        return result

    def scatter_sent(s, kind, j):
        @pl.when(end_chip)
        def _():
            scatter(s, kind, j, over_chip, OVER).wait_send()
            scatter(s, kind, j, near_chip, NEAR).wait_send()

        @pl.when(middle_chip)
        def _():
            scatter(s, kind, j, across_chip, ACROSS).wait_send()

    own_rows = (r.nrm, r.nmlp, r.ups, r.brn, r.act, r.gpre, r.mix, r.dqkv)
    all_rows = (
        r.all_nrm,
        r.all_nmlp,
        r.all_ups,
        r.all_brn,
        r.all_act,
        r.all_gpre,
        r.all_mix,
        r.all_dqkv,
    )

    def rows_copy(index, s, same, stays=False):
        core = c if same else 1 - c
        src = own_rows[index].at[s]
        dst = all_rows[index].at[a, c]
        if index <= BRN:
            src = src.at[:, :, row_block(core, half_width)]
        recv = r.rows_r.at[index]
        if stays:
            return pltpu.make_async_copy(src, dst, recv)
        if same:
            return remote(src, dst, r.rows_s.at[index, s, 0], recv, section=s)
        return remote(src, dst, r.rows_s.at[index, s, 1], recv, section=s, seq=1 - c)

    def rows_start(index, s):
        @pl.when(a == s)
        def _():
            rows_copy(index, s, True, True).start()

        @pl.when(a != s)
        def _():
            rows_copy(index, s, True).start()

        if index <= BRN:
            rows_copy(index, s, False).start()

    def forward_rows(s):
        for index in (NRM, MIX, NMLP, ACT):
            rows_start(index, s)

    def rows_sent(index, s):
        @pl.when(a != s)
        def _():
            rows_copy(index, s, True).wait_send()

        if index <= BRN:
            rows_copy(index, s, False).wait_send()

    def share_copy(index, core):
        view = all_rows[index].at[:, core]
        return remote(view, view, r.share_s.at[index - ACT], r.share_r.at[index - ACT], seq=1 - c)

    def share(index):
        drain(all_rows[index].at[:, c], r.rows_r.at[index])
        share_copy(index, c).start()

    def norm_copy(s):
        return remote(
            r.norm_part.at[s], r.norm_all.at[a], r.norm_s.at[s], r.norm_r, section=s
        )

    def norm_start(s):
        @pl.when(a == s)
        def _():
            pltpu.make_async_copy(r.norm_part.at[s], r.norm_all.at[a], r.norm_r).start()

        @pl.when(a != s)
        def _():
            norm_copy(s).start()

    def home_copy(what, s, j):
        src, dst, send, recv = what
        chip = 2 * j + t - 1
        return remote(src.at[s, j], dst.at[a], send.at[s, j], recv, section=s, tensor=chip)

    def home_start(what, s):
        @pl.when(middle_chip)
        def _():
            for j in streams:
                home_copy(what, s, j).start()

    def home_sent(what, s):
        @pl.when(middle_chip)
        def _():
            for j in streams:
                home_copy(what, s, j).wait_send()

    out_home = (r.out_low, r.acts, r.out_s, r.out_r)
    grad_home = (r.grad_low, r.grads, r.grad_s, r.grad_r)

    length = r.lengths[a // buckets, a % buckets]
    key = iota((stream_rows, total), 1)
    for j in streams:
        query = c * local + j * stream_rows + iota((stream_rows, total), 0)
        r.near[j] = jnp.where((query >= key) & (query - key < WIN), 1.0, 0.0)
    key_row = iota((1, total), 1)

    def row_mask(place):
        return jnp.where(place < length, 1.0, 0.0)

    def stream_mask(j):
        return row_mask(c * local + j * stream_rows + iota((stream_rows, 1), 0))

    def multiplicity(s, j, head):
        block = j * stream_rows // QB
        pick = head * blocks + block
        limit = (c * blocks + block) * QB - WIN
        return r.near[j] + jnp.where(key_row <= limit, r.count[s, pick : pick + 1, :], 0.0)

    def head_cols(head):
        return slice(head * HDIM, (head + 1) * HDIM)

    def kv_copy(s, j):
        view = r.kv.at[s, :, j * stream_rows : (j + 1) * stream_rows]
        return remote(view, view, r.kv_s.at[s, j], r.kv_r.at[s, j], seq=1 - c)

    def dkv_copy(s):
        return remote(r.dkv_out.at[s], r.dkv_in.at[s], r.dkv_s.at[s], r.dkv_r.at[s], seq=1 - c)

    def own_sequence(ref):
        both = ref[a // buckets].astype(F32)
        picked = both[:, 0, :]
        for bucket in range(1, buckets):
            picked = jnp.where(a % buckets == bucket, both[:, bucket, :], picked)
        return picked

    def first_copy(stream):
        return remote(
            r.first_out, r.first_in.at[stream], r.first_s, r.first_r.at[stream], tensor=1 + t % 2
        )

    own_place = c * local + t * rows + iota((rows, 1), 0)
    r.first_out[0] = own_sequence(r.inputs).astype(LOW)
    r.first_out[1] = (own_sequence(r.cotangent) * row_mask(own_place)).astype(LOW)
    first_copy(t // 2).start()
    r.norm_part[...] = jnp.zeros_like(r.norm_part)

    def first_rows(j):
        @pl.when(middle_chip)
        def _():
            first_copy(j).wait_recv()
            r.hidden[j] = r.first_in[j, 0].astype(F32)
            r.upstream[j] = r.first_in[j, 1]

    def on_owner(stage):
        def run(s, j):
            @pl.when(middle_chip)
            def _():
                stage(s, j)

        return run

    @on_owner
    def enter(s, j):
        xhat, inverse = standard(r.hidden[j])
        r.xhat1[s, j] = xhat
        r.inv1[s, j] = jnp.broadcast_to(inverse, (owned, 128))
        r.nrm[s, j, mine] = (xhat * r.small[s, 0:1] + r.small[s, 1:2]).astype(LOW)
        gather_start(r.nrm, s, 0, j)

    def project(s, j):
        gather_wait(r.nrm, s, 0, j)
        normed = r.nrm[s, j]
        place = row_block(c * STREAMS + j, stream_rows)
        bias_v = r.small[s, 7:8, half_width : half_width + head_width]
        key_rows = dot_nt(normed, r.wq[s, head_width : 2 * head_width])
        value_rows = dot_nt(normed, r.wq[s, 2 * head_width : 3 * head_width]) + bias_v
        r.kv[s, 0, place] = key_rows.astype(LOW)
        r.kv[s, 1, place] = value_rows.astype(LOW)

    def ask(s, j):
        queries = dot_nt(r.nrm[s, j], r.wq[s, 0:head_width]) + r.small[s, 7:8, :head_width]
        r.qry[s, j] = queries.astype(LOW)

    def attend_line(s, j):
        mixed = []
        for head in range(heads):
            cols = head_cols(head)
            times = multiplicity(s, j, head)
            scores = scale * dot_nt(r.qry[s, j, :, cols], r.kv[s, 0, :, cols])
            scores = jnp.where(times > 0.0, scores, MASKED)
            top = jnp.max(scores, axis=-1, keepdims=True)
            terms = times * jnp.exp(scores - top)
            weights = terms / jnp.sum(terms, axis=-1, keepdims=True)
            r.soft[s, j, head] = weights
            mixed.append(dot_nn(weights.astype(LOW), r.kv[s, 1, :, cols]))
        r.mix[s, j] = (jnp.concatenate(mixed, axis=-1) * stream_mask(j)).astype(LOW)

    def leave_attention(s, j):
        scatter_start(s, 0, j, dot_nn(r.mix[s, j], r.wo[s]))

    @on_owner
    def between(s, j):
        middle = r.hidden[j] + scatter_sum(s, 0, j) + r.small[s, 4:5]
        r.middle[j] = middle
        xhat, inverse = standard(middle)
        r.xhat2[s, j] = xhat
        r.inv2[s, j] = jnp.broadcast_to(inverse, (owned, 128))
        r.nmlp[s, j, mine] = (xhat * r.small[s, 2:3] + r.small[s, 3:4]).astype(LOW)
        gather_start(r.nmlp, s, 1, j)

    def feed(s, j):
        gather_wait(r.nmlp, s, 1, j)
        before = dot_nn(r.nmlp[s, j], r.wf[s]) + r.small[s, 6:7, :units]
        bend = jnp.tanh(0.7978845608028654 * (before + 0.044715 * before * before * before))
        r.act[s, j] = (0.5 * before * (1.0 + bend)).astype(LOW)
        r.slope[s, j] = 0.5 * (1.0 + bend) + 0.5 * before * (1.0 - bend * bend) * (
            0.7978845608028654 * (1.0 + 3 * 0.044715 * before * before)
        )


    def leave_feed(s, j):
        scatter_start(s, 1, j, dot_nn(r.act[s, j], r.wp[s]))

    @on_owner
    def finish(s, j):
        result = r.middle[j] + scatter_sum(s, 1, j) + r.small[s, 5:6]
        r.out_low[s, j] = result.astype(LOW)
        r.hidden[j] = result.astype(LOW).astype(F32)

    def small_ready(s):
        @pl.when(a != s)
        def _():
            small_copy(0, a, s).wait_recv()

    small_ready(0)
    for j in streams:
        first_rows(j)
        enter(0, j)

    def forward(s, _):
        need(s, 0)
        need(s, 1)

        @pl.when(a != s)
        def _():
            count_copy(0, a, s).wait_recv()

        for j in streams:
            project(s, j)

            @pl.when(c == 0)
            def _():
                kv_copy(s, j).start()

            ask(s, j)
            if j == 0:

                @pl.when(c == 1)
                def _():
                    for other in streams:
                        kv_copy(s, other).wait_recv()

            attend_line(s, j)
            leave_attention(s, j)

        @pl.when(s == 0)
        def _():
            pass_all(0, (2,))
            for later in range(1, lines):
                pass_all(later, (0, 1, 2))

        @pl.when(s == 1)
        def _():
            pass_far(1, 2)
            pass_far(1, 3)
            for later in range(2, lines):
                for p in range(4):
                    pass_far(later, p)

        for j in streams:
            between(s, j)
        @pl.when(s == 0)
        def _():
            for later in range(lines):
                pass_all(later, (3,))

        need(s, 2)
        for j in streams:
            feed(s, j)
            if j == 0:
                need(s, 3)
            leave_feed(s, j)


        @pl.when(s >= 2)
        def _():
            forward_rows(s - 2)


        @pl.when(s + 1 < lines)
        def _():
            small_ready(s + 1)

        for j in streams:
            finish(s, j)

            @pl.when(s + 1 < lines)
            def _():
                enter(s + 1, j)

        home_start(out_home, s)

        @pl.when(s == 0)
        def _():
            pass_far(1, 0)
            pass_far(1, 1)

        return 0

    lax.fori_loop(0, lines, forward, 0)

    @on_owner
    def turn(s, j):
        upstream = r.upstream[j]
        r.ups[s, j, mine] = upstream
        gather_start(r.ups, s, 2, j)
        r.norm_part[s, 5:6] += column_sum(upstream)

    def feed_back(s, j):
        gather_wait(r.ups, s, 2, j)
        grad_pre = (dot_nt(r.ups[s, j], r.wp[s]) * r.slope[s, j]).astype(LOW)
        r.gpre[s, j] = grad_pre
        scatter_start(s, 2, j, dot_nt(grad_pre, r.wf[s]))
        r.norm_part[s, 6:7, :units] += column_sum(grad_pre)

    @on_owner
    def between_back(s, j):
        grad = scatter_sum(s, 2, j)
        xhat = r.xhat2[s, j]
        upstream = r.upstream[j].astype(F32)
        grad_middle = upstream + standard_back(
            grad * r.small[s, 2:3], xhat, r.inv2[s, j, :, 0:1]
        )
        r.middle[j] = grad_middle
        branch = grad_middle.astype(LOW)
        r.brn[s, j, mine] = branch
        gather_start(r.brn, s, 3, j)
        r.norm_part[s, 2:3] += column_sum(grad * xhat)
        r.norm_part[s, 3:4] += column_sum(grad)
        r.norm_part[s, 4:5] += column_sum(branch)

    def mixed_back(s, j):
        gather_wait(r.brn, s, 3, j)
        r.gmix[j] = (dot_nt(r.brn[s, j], r.wo[s]) * stream_mask(j)).astype(LOW)

    def attend_line_back(s, j):
        grad_q, grad_k, grad_v = [], [], []
        for head in range(heads):
            cols = head_cols(head)
            weights = r.soft[s, j, head]
            grad_head = r.gmix[j, :, cols]
            grad_weights = dot_nt(grad_head, r.kv[s, 1, :, cols])
            inner = jnp.sum(weights * grad_weights, axis=-1, keepdims=True)
            grad_scores = (weights * (grad_weights - inner)).astype(LOW)
            grad_k.append(scale * dot_tn(grad_scores, r.qry[s, j, :, cols]))
            grad_v.append(dot_tn(weights.astype(LOW), grad_head))
            grad_q.append(scale * dot_nn(grad_scores, r.kv[s, 0, :, cols]))
        for which, grad in enumerate((grad_k, grad_v)):
            grad = jnp.concatenate(grad, axis=-1)
            r.dkv_all[which] = grad if j == STREAMS - 1 else r.dkv_all[which] + grad
        grad_q = jnp.concatenate(grad_q, axis=-1).astype(LOW)
        r.dqkv[s, 0, j] = grad_q
        r.norm_part[s, 7:8, :head_width] += column_sum(grad_q)

    def join_keys(s, j):
        for which in range(2):
            joined = r.dkv_all[which, row_block(c * STREAMS + j, stream_rows)].astype(LOW)
            r.dqkv[s, 1 + which, j] = joined
            if which == 1:
                lanes = slice(half_width, half_width + head_width)
                r.norm_part[s, 7:8, lanes] += column_sum(joined)

    def leave_back(s, j):
        product = dot_nn(r.dqkv[s, 0, j], r.wq[s, 0:head_width])
        for which in range(1, 3):
            weight = r.wq[s, which * head_width : (which + 1) * head_width]
            product = product + dot_nn(r.dqkv[s, which, j], weight)
        scatter_start(s, 3, j, product)

    @on_owner
    def finish_back(s, j):
        grad = scatter_sum(s, 3, j)
        xhat = r.xhat1[s, j]
        result = r.middle[j] + standard_back(
            grad * r.small[s, 0:1], xhat, r.inv1[s, j, :, 0:1]
        )
        r.upstream[j] = result.astype(LOW)
        r.grad_low[s, j] = result.astype(LOW)
        r.norm_part[s, 0:1] += column_sum(grad * xhat)
        r.norm_part[s, 1:2] += column_sum(grad)

    last_first = tuple(reversed(streams))
    for j in last_first:
        turn(lines - 1, j)

    def backward(index, _):
        s = lines - 1 - index
        for j in last_first:
            feed_back(s, j)
        rows_start(UPS, s)
        rows_start(GPRE, s)

        @pl.when(index < 2)
        def _():
            forward_rows(lines - 2 + index)

        @pl.when(index == lines - 1)
        def _():
            share(ACT)
            share(MIX)

        for j in last_first:
            between_back(s, j)
        for j in last_first:
            mixed_back(s, j)
            attend_line_back(s, j)

            @pl.when(c == 1)
            def _():
                join_keys(s, j)
                leave_back(s, j)

        rows_start(BRN, s)

        @pl.when(c == 1)
        def _():
            r.dkv_out[s] = r.dkv_all[:, 0:local].astype(LOW)
            dkv_copy(s).start()

        @pl.when(c == 0)
        def _():
            dkv_copy(s).wait_recv()
            r.dkv_all[:, 0:local] += r.dkv_in[s].astype(F32)
            for j in last_first:
                join_keys(s, j)
                leave_back(s, j)

        rows_start(DQKV, s)
        for j in last_first:
            finish_back(s, j)

            @pl.when(s > 0)
            def _():
                turn(s - 1, j)

        norm_start(s)
        home_start(grad_home, s)
        return 0

    lax.fori_loop(0, lines, backward, 0)

    share(GPRE)
    share(DQKV)

    drain(r.norm_all, r.norm_r)
    slot = c * chips + t
    norm_sum = r.norm_all[0]
    for line in range(1, lines):
        norm_sum = norm_sum + r.norm_all[line]
    r.ends[slot] = norm_sum

    def ends_copy(step):
        core, chip = step // chips, step % chips
        view = r.ends.at[slot]
        return remote(
            view,
            view,
            r.ends_s.at[step - 1],
            r.ends_r,
            seq=(c + core) % 2,
            tensor=(t + chip) % chips,
        )

    for step in range(1, 2 * chips):
        ends_copy(step).start()

    for kind, buffer in enumerate((r.nrm, r.nmlp, r.ups, r.brn)):
        for j in streams:
            scatter_sent(0, kind, j)

            @pl.when(middle_chip)
            def _():
                gather_sent(buffer, 0, kind, j)

    for index in range(ACT):
        drain(all_rows[index], r.rows_r.at[index])
    for index in range(ACT, 8):
        share_copy(index, 1 - c).wait_recv()
        share_copy(index, c).wait_send()
    drain(r.acts, r.out_r)
    drain(r.grads, r.grad_r)
    drain(r.ends.at[0 : 2 * chips - 1], r.ends_r)
    for step in range(1, 2 * chips):
        ends_copy(step).wait_send()
    for step in range(1, lines):
        small_copy(step - 1, (a + step) % lines, a).wait_send()
        count_copy(step - 1, (a + step) % lines, a).wait_send()
    for p in range(4):
        for which, line in enumerate((beside(a), above(a))):
            first_hop(p, a, line, which).wait_send()

    first_copy(t // 2).wait_send()

    def sent(s, _):
        home_sent(out_home, s)
        home_sent(grad_home, s)

        @pl.when(a != s)
        def _():
            norm_copy(s).wait_send()

        @pl.when(c == 0)
        def _():
            for j in streams:
                kv_copy(s, j).wait_send()

        @pl.when(c == 1)
        def _():
            dkv_copy(s).wait_send()

        for index in range(8):
            rows_sent(index, s)
        for p in range(4):

            @pl.when((a == beside(s)) | (a == above(s)))
            def _():
                second_hop(p, s, 0).wait_send()

            @pl.when(a != s)
            def _():
                core_hop(p, s, c).wait_send()

        return 0

    lax.fori_loop(0, lines, sent, 0)


def relay_call(inputs, cotangent, lengths, chosen, singles, weights):
    lines = lax.axis_size("section")
    chips = lax.axis_size("tensor")
    rows, buckets, width = inputs.shape[1:]
    local, total, half = rows * chips, 2 * rows * chips, width // 2
    head_width, units = weights["wo_in"].shape[0], weights["wp_in"].shape[0]
    heads = head_width // HDIM
    stream = local // STREAMS
    peers, owned = chips - 1, stream // 2
    vmem, dma = pltpu.VMEM, pltpu.SemaphoreType.DMA
    operands = dict(
        inputs=inputs,
        cotangent=cotangent,
        lengths=lengths,
        chosen=chosen,
        **singles,
        **weights,
    )

    def space(name):
        if name in weights:
            return pl.ANY
        return pltpu.SMEM if operands[name] is lengths else pltpu.VMEM

    sums = dict(
        acts=((lines, rows, width), LOW),
        grads=((lines, rows, width), LOW),
        ends=((2 * chips, 8, width), F32),
    )
    gathered = dict(
        all_nrm=((lines, 2, STREAMS, stream, half), LOW),
        all_nmlp=((lines, 2, STREAMS, stream, half), LOW),
        all_ups=((lines, 2, STREAMS, stream, half), LOW),
        all_brn=((lines, 2, STREAMS, stream, half), LOW),
        all_act=((lines, 2, STREAMS, stream, units), LOW),
        all_gpre=((lines, 2, STREAMS, stream, units), LOW),
        all_mix=((lines, 2, STREAMS, stream, head_width), LOW),
        all_dqkv=((lines, 2, 3, STREAMS, stream, head_width), LOW),
    )
    outputs = dict(**sums, **gathered)
    scratch = dict(
        wq=vmem((lines,) + weights["wq_in"].shape, LOW),
        wo=vmem((lines,) + weights["wo_in"].shape, LOW),
        wf=vmem((lines,) + weights["wf_in"].shape, LOW),
        wp=vmem((lines,) + weights["wp_in"].shape, LOW),
        small_own=vmem((8, width), F32),
        small=vmem((lines, 8, width), F32),
        count_own=vmem((lines, 8, total), F32),
        count=vmem((lines, 8, total), F32),
        hidden=vmem((STREAMS, owned, width), F32),
        middle=vmem((STREAMS, owned, width), F32),
        upstream=vmem((STREAMS, owned, width), LOW),
        first_out=vmem((2, owned, width), LOW),
        first_in=vmem((STREAMS, 2, owned, width), LOW),
        xhat1=vmem((lines, STREAMS, owned, width), F32),
        inv1=vmem((lines, STREAMS, owned, 128), F32),
        xhat2=vmem((lines, STREAMS, owned, width), F32),
        inv2=vmem((lines, STREAMS, owned, 128), F32),
        nrm=vmem((lines, STREAMS, stream, width), LOW),
        nmlp=vmem((lines, STREAMS, stream, width), LOW),
        ups=vmem((lines, STREAMS, stream, width), LOW),
        brn=vmem((lines, STREAMS, stream, width), LOW),
        act=vmem((lines, STREAMS, stream, units), LOW),
        gpre=vmem((lines, STREAMS, stream, units), LOW),
        slope=vmem((lines, STREAMS, stream, units), F32),
        mix=vmem((lines, STREAMS, stream, head_width), LOW),
        qry=vmem((lines, STREAMS, stream, head_width), LOW),
        gmix=vmem((STREAMS, stream, head_width), LOW),
        dqkv=vmem((lines, 3, STREAMS, stream, head_width), LOW),
        kv=vmem((lines, 2, total, head_width), LOW),
        soft=vmem((lines, STREAMS, heads, stream, total), F32),
        near=vmem((STREAMS, stream, total), F32),
        dkv_all=vmem((2, total, head_width), F32),
        dkv_out=vmem((lines, 2, local, head_width), LOW),
        dkv_in=vmem((lines, 2, local, head_width), LOW),
        part=vmem((4, STREAMS, stream, width), LOW),
        arrived=vmem((lines, 4, STREAMS, peers, owned, width), LOW),
        out_low=vmem((lines, STREAMS, owned, width), LOW),
        grad_low=vmem((lines, STREAMS, owned, width), LOW),
        norm_part=vmem((lines, 8, width), F32),
        norm_all=vmem((lines, 8, width), F32),
        w_first_s=dma((4, 2)),
        w_first_r=dma((lines, 4)),
        w_second_s=dma((lines, 4)),
        w_second_r=dma((lines, 4, 2)),
        w_core_s=dma((lines, 4)),
        w_core_r=dma((lines, 4)),
        w_own=dma((4,)),
        small_s=dma((lines - 1,)),
        small_r=dma((lines,)),
        count_s=dma((lines - 1,)),
        count_r=dma((lines,)),
        ag_s=dma((4, STREAMS, peers)),
        ag_r=dma((4, STREAMS, peers)),
        rs_s=dma((4, STREAMS, peers)),
        rs_r=dma((4, STREAMS, peers)),
        kv_s=dma((lines, STREAMS)),
        kv_r=dma((lines, STREAMS)),
        dkv_s=dma((lines,)),
        dkv_r=dma((lines,)),
        rows_s=dma((8, lines, 2)),
        rows_r=dma((8,)),
        share_s=dma((4,)),
        share_r=dma((4,)),
        first_s=dma,
        first_r=dma((STREAMS,)),
        out_s=dma((lines, STREAMS)),
        out_r=dma,
        grad_s=dma((lines, STREAMS)),
        grad_r=dma,
        norm_s=dma((lines,)),
        norm_r=dma,
        ends_s=dma((2 * chips - 1,)),
        ends_r=dma,
    )
    names = tuple(operands) + tuple(outputs) + tuple(scratch)
    results = pl.pallas_call(
        functools.partial(relay_kernel, names),
        out_shape=[jax.ShapeDtypeStruct(shape, kind) for shape, kind in outputs.values()],
        in_specs=[pl.BlockSpec(memory_space=space(name)) for name in operands],
        out_specs=[
            pl.BlockSpec(memory_space=pl.ANY if name in gathered else pltpu.VMEM)
            for name in outputs
        ],
        scratch_shapes=list(scratch.values()),
        compiler_params=pltpu.CompilerParams(
            collective_id=0, has_side_effects=True, vmem_limit_bytes=60 * 2**20
        ),
        name="relay",
    )(*operands.values())
    return dict(zip(outputs, results))


def weights_kernel(names, *refs):
    r = types.SimpleNamespace(**dict(zip(names, refs)))
    step = pl.program_id(0)
    micro_count, rows, buckets, width = r.activations.shape
    chips, units, head_width = r.ends.shape[0] // 2, r.all_act.shape[-1], r.all_mix.shape[-1]

    @pl.when(step == 0)
    def _():
        sums = r.ends[0]
        for other in range(1, 2 * chips):
            sums = sums + r.ends[other]
        singles = (r.ln1_gain, r.ln1_shift, r.ln2_gain, r.ln2_shift, r.b_out, r.b_proj)
        for place, single in enumerate(singles):
            single[...] = sums[place : place + 1]
        for chip in range(chips):
            both = r.ends[chip] + r.ends[chips + chip]
            r.b_fc[:, chip * units : (chip + 1) * units] = both[6:7, :units]
            here = slice(chip * head_width, (chip + 1) * head_width)
            r.b_qv[0:1, here] = both[7:8, :head_width]
            r.b_qv[1:2, here] = both[7:8, width // 2 : width // 2 + head_width]
        for target, source in ((r.activations, r.acts), (r.in_grads, r.grads)):
            for micro in range(micro_count):
                rows_of = [
                    source[micro * buckets + bucket].astype(F32)[:, None, :]
                    for bucket in range(buckets)
                ]
                target[micro] = jnp.concatenate(rows_of, axis=1).astype(LOW)
        for target in (r.w_qkv, r.w_out, r.w_fc, r.w_proj):
            target[...] = jnp.zeros_like(target)

    def rows_of_sequence(ref):
        return ref[0].reshape(2 * chips * rows, ref.shape[-1])

    nrm, nmlp, ups, brn, act, gpre, mix = (
        rows_of_sequence(ref)
        for ref in (r.all_nrm, r.all_nmlp, r.all_ups, r.all_brn, r.all_act, r.all_gpre, r.all_mix)
    )
    r.w_proj[...] += dot_tn(act, ups)
    r.w_fc[...] += dot_tn(nmlp, gpre)
    r.w_out[...] += dot_tn(mix, brn)
    for which in range(3):
        grad = r.all_dqkv[0, :, which].reshape(2 * chips * rows, head_width)
        r.w_qkv[which] += dot_tn(grad, nrm)


def weights_call(relayed, inputs_shape, head_width, units):
    lines = lax.axis_size("section")
    chips = lax.axis_size("tensor")
    width = inputs_shape[-1]
    half = width // 2
    outputs = dict(
        activations=(inputs_shape, LOW),
        in_grads=(inputs_shape, LOW),
        ln1_gain=((1, width), F32),
        ln1_shift=((1, width), F32),
        w_qkv=((3, head_width, half), F32),
        b_qv=((2, width), F32),
        w_out=((head_width, half), F32),
        b_out=((1, width), F32),
        ln2_gain=((1, width), F32),
        ln2_shift=((1, width), F32),
        w_fc=((half, units), F32),
        b_fc=((1, chips * units), F32),
        w_proj=((units, half), F32),
        b_proj=((1, width), F32),
    )

    def spec(array):
        if len(array.shape) < 5:
            return pl.BlockSpec(array.shape, lambda step: (0,) * len(array.shape))
        return pl.BlockSpec(
            (1,) + array.shape[1:], lambda step: (step,) + (0,) * (len(array.shape) - 1)
        )

    def whole(shape):
        return pl.BlockSpec(shape, lambda step: (0,) * len(shape))

    return pl.pallas_call(
        functools.partial(weights_kernel, tuple(relayed) + tuple(outputs)),
        out_shape=[jax.ShapeDtypeStruct(shape, kind) for shape, kind in outputs.values()],
        grid=(lines,),
        in_specs=[spec(array) for array in relayed.values()],
        out_specs=[whole(shape) for shape, _ in outputs.values()],
        compiler_params=pltpu.CompilerParams(vmem_limit_bytes=60 * 2**20),
        name="weight_gradients",
    )(*relayed.values())


def on_line(
    inputs,
    cotangent,
    lengths,
    chosen,
    ln1_gain,
    ln1_shift,
    w_qkv,
    b_qv,
    w_out,
    b_out,
    ln2_gain,
    ln2_shift,
    w_fc,
    b_fc,
    w_proj,
    b_proj,
):
    head_width, units = w_out.shape[1], w_fc.shape[2]
    singles = dict(
        ln1_gain=ln1_gain,
        ln1_shift=ln1_shift,
        ln2_gain=ln2_gain,
        ln2_shift=ln2_shift,
        b_out=b_out,
        b_proj=b_proj,
        b_fc=b_fc,
        b_qv=b_qv[0],
    )
    weights = dict(
        wq_in=jnp.swapaxes(w_qkv[0], 1, 2).reshape(-1, inputs.shape[-1]),
        wo_in=w_out[0],
        wf_in=w_fc[0],
        wp_in=w_proj[0],
    )
    picks = chosen.reshape((-1,) + chosen.shape[-2:])
    relayed = relay_call(inputs, cotangent, lengths, picks, singles, weights)
    results = list(weights_call(relayed, inputs.shape, head_width, units))
    results[4] = jnp.swapaxes(results[4], 1, 2)
    vectors = (2, 3, 7, 8, 9, 11, 13)
    return tuple(
        result if place in vectors else result[None] for place, result in enumerate(results)
    )


def fits_lines(mesh):
    return mesh.shape["section"] == 4 and mesh.shape["seq"] == 2 and mesh.shape["tensor"] == 4


def solution(mesh):
    placed = (
        P(None, ("seq", "tensor"), None, None),
        P(None, ("seq", "tensor"), None, None),
        P(),
        P("section", None, None, "tensor", "seq", None),
        P("section", None),
        P("section", None),
        P("section", None, None, "tensor"),
        P("section", None, "tensor"),
        P("section", "tensor", None),
        P("section", None),
        P("section", None),
        P("section", None),
        P("section", None, "tensor"),
        P("section", "tensor"),
        P("section", "tensor", None),
        P("section", None),
    )
    return jax.shard_map(
        on_line if fits_lines(mesh) else on_device,
        mesh=mesh,
        in_specs=placed,
        out_specs=(
            P("section", None, ("seq", "tensor"), None, None),
            P("section", None, ("seq", "tensor"), None, None),
            P("section", None),
            P("section", None),
            P("section", None, "seq", "tensor"),
            P("section", None, None),
            P("section", "tensor", "seq"),
            P("section", None),
            P("section", None),
            P("section", None),
            P("section", "seq", "tensor"),
            P("section", None),
            P("section", "tensor", "seq"),
            P("section", None),
        ),
        check_vma=False,
    )
```

profile of v0, /device:TPU:1, one launch (start us, length us, event | category | flops | bytes accessed | tf_op | source)
XLA Modules:
  0.0 258.2 jit_solution(10613034376829682384)
XLA Ops:
  0.7 248.7 %relay.1 = (bf16[4,32,768]{2,1,0:T(8,128)(2,1)}, bf16[4,32,768]{2,1,0:T(8,128)(2,1)}, f32[8,8,768]{2,1,0:T(8,128)}, bf16[4,2,2,64,384]{4,3,2,1,0:T(8,128)(2,1)},...) custom-call(bf16[2,32,2,768]{3,2,1,0:T(2,128)(2,1)} %refs_0_.1, ...), custom_call_target="tpu_custom_call" | custom-call | tf_op jit(solution)/shard_map/relay/pallas_call | solution.py:1504
  249.3 8.8 %weight_gradients.1 = (bf16[2,32,2,768]{3,2,1,0:T(2,128)(2,1)}, bf16[2,32,2,768]{3,2,1,0:T(2,128)(2,1)}, f32[1,768]{1,0:T(1,128)}, f32[1,768]{1,0:T(1,128)}, f32...) custom-call(bf16[4,32,768]{2,1,0:T(8,128)(2,1)} %get-tuple-element.3, ...), custom_call_target="tpu_custom_call" | custom-call | tf_op jit(solution)/shard_map/weight_gradients/pallas_call | solution.py:1598
where the time goes:
time: 258 us
  Pallas kernels  257 us (100%)
    pallas_call x1, Pallas kernels, relay_call(): pl.pallas_call(functools.partial(relay_kernel, names), out_shape=[jax.Sha...  249 us
    pallas_call x1, Pallas kernels, weights_call(): pl.pallas_call(functools.partial(weights_kernel, tuple(relayed) + tuple(o...  8.83 us

commit v1 on v0

--- a/solution.py
+++ b/solution.py
@@ -864,40 +864,90 @@
         dst = all_rows[index].at[a, c]
         if index <= BRN:
             src = src.at[:, :, row_block(core, half_width)]
-        recv = r.rows_r.at[index]
+        recv = r.heads_r.at[a] if index == DQKV else r.rows_r.at[index]
         if stays:
             return pltpu.make_async_copy(src, dst, recv)
         if same:
             return remote(src, dst, r.rows_s.at[index, s, 0], recv, section=s)
         return remote(src, dst, r.rows_s.at[index, s, 1], recv, section=s, seq=1 - c)
 
+    passed_rows = {UPS: r.pass_ups, GPRE: r.pass_gpre}
+    places = {UPS: 0, GPRE: 1}
+
+    def detour_copy(index):
+        return remote(
+            own_rows[index].at[0],
+            passed_rows[index],
+            r.pass_s.at[places[index]],
+            r.pass_r.at[places[index]],
+            section=1,
+        )
+
+    def passed_copies(index):
+        copies = []
+        for step in range(2 if index <= BRN else 1):
+            core = (c + step) % 2
+            src = passed_rows[index]
+            if index <= BRN:
+                src = src.at[:, :, row_block(core, half_width)]
+            send = r.pass_on_s.at[places[index], step]
+            dst = all_rows[index].at[3, c]
+            copies.append(remote(src, dst, send, r.rows_r.at[index], section=0, seq=core))
+        return copies
+
+    def pass_rows(index):
+        @pl.when(a == 1)
+        def _():
+            detour_copy(index).wait_recv()
+            for copy in passed_copies(index):
+                copy.start()
+
+    def goes_direct(index, s):
+        return jnp.logical_not((a == 3) & (s == 0)) if index in passed_rows else a >= 0
+
     def rows_start(index, s):
+        if index in passed_rows:
+
+            @pl.when((a == 3) & (s == 0))
+            def _():
+                detour_copy(index).start()
+
         @pl.when(a == s)
         def _():
             rows_copy(index, s, True, True).start()
 
-        @pl.when(a != s)
+        @pl.when((a != s) & goes_direct(index, s))
         def _():
             rows_copy(index, s, True).start()
 
         if index <= BRN:
-            rows_copy(index, s, False).start()
+
+            @pl.when(goes_direct(index, s))
+            def _():
+                rows_copy(index, s, False).start()
 
     def forward_rows(s):
         for index in (NRM, MIX, NMLP, ACT):
             rows_start(index, s)
 
     def rows_sent(index, s):
-        @pl.when(a != s)
+        @pl.when((a != s) & goes_direct(index, s))
         def _():
             rows_copy(index, s, True).wait_send()
 
         if index <= BRN:
-            rows_copy(index, s, False).wait_send()
+
+            @pl.when(goes_direct(index, s))
+            def _():
+                rows_copy(index, s, False).wait_send()
 
     def share_copy(index, core):
         view = all_rows[index].at[:, core]
         return remote(view, view, r.share_s.at[index - ACT], r.share_r.at[index - ACT], seq=1 - c)
+
+    def share_heads(line, core):
+        view = r.all_dqkv.at[line, core]
+        return remote(view, view, r.heads_s.at[line], r.heads_sr.at[line], seq=1 - c)
 
     def share(index):
         drain(all_rows[index].at[:, c], r.rows_r.at[index])
@@ -1263,14 +1313,14 @@
             between_back(s, j)
         for j in last_first:
             mixed_back(s, j)
+            if j == 0:
+                rows_start(BRN, s)
             attend_line_back(s, j)
 
             @pl.when(c == 1)
             def _():
                 join_keys(s, j)
                 leave_back(s, j)
-
-        rows_start(BRN, s)
 
         @pl.when(c == 1)
         def _():
@@ -1286,6 +1336,12 @@
                 leave_back(s, j)
 
         rows_start(DQKV, s)
+
+        @pl.when(s == 0)
+        def _():
+            pass_rows(UPS)
+            pass_rows(GPRE)
+
         for j in last_first:
             finish_back(s, j)
 
@@ -1300,7 +1356,9 @@
     lax.fori_loop(0, lines, backward, 0)
 
     share(GPRE)
-    share(DQKV)
+    for line in range(lines):
+        drain(r.all_dqkv.at[line, c], r.heads_r.at[line])
+        share_heads(line, c).start()
 
     drain(r.norm_all, r.norm_r)
     slot = c * chips + t
@@ -1324,6 +1382,17 @@
     for step in range(1, 2 * chips):
         ends_copy(step).start()
 
+    for index in (UPS, GPRE):
+
+        @pl.when(a == 3)
+        def _():
+            detour_copy(index).wait_send()
+
+        @pl.when(a == 1)
+        def _():
+            for copy in passed_copies(index):
+                copy.wait_send()
+
     for kind, buffer in enumerate((r.nrm, r.nmlp, r.ups, r.brn)):
         for j in streams:
             scatter_sent(0, kind, j)
@@ -1334,9 +1403,12 @@
 
     for index in range(ACT):
         drain(all_rows[index], r.rows_r.at[index])
-    for index in range(ACT, 8):
+    for index in range(ACT, DQKV):
         share_copy(index, 1 - c).wait_recv()
         share_copy(index, c).wait_send()
+    for line in range(lines):
+        share_heads(line, 1 - c).wait_recv()
+        share_heads(line, c).wait_send()
     drain(r.acts, r.out_r)
     drain(r.grads, r.grad_r)
     drain(r.ends.at[0 : 2 * chips - 1], r.ends_r)
@@ -1454,6 +1526,8 @@
         qry=vmem((lines, STREAMS, stream, head_width), LOW),
         gmix=vmem((STREAMS, stream, head_width), LOW),
         dqkv=vmem((lines, 3, STREAMS, stream, head_width), LOW),
+        pass_ups=vmem((STREAMS, stream, width), LOW),
+        pass_gpre=vmem((STREAMS, stream, units), LOW),
         kv=vmem((lines, 2, total, head_width), LOW),
         soft=vmem((lines, STREAMS, heads, stream, total), F32),
         near=vmem((STREAMS, stream, total), F32),
@@ -1487,8 +1561,14 @@
         dkv_r=dma((lines,)),
         rows_s=dma((8, lines, 2)),
         rows_r=dma((8,)),
+        pass_s=dma((2,)),
+        pass_r=dma((2,)),
+        pass_on_s=dma((2, 2)),
         share_s=dma((4,)),
         share_r=dma((4,)),
+        heads_r=dma((lines,)),
+        heads_s=dma((lines,)),
+        heads_sr=dma((lines,)),
         first_s=dma,
         first_r=dma((STREAMS,)),
         out_s=dma((lines, STREAMS)),
@@ -1520,51 +1600,84 @@
 
 def weights_kernel(names, *refs):
     r = types.SimpleNamespace(**dict(zip(names, refs)))
-    step = pl.program_id(0)
     micro_count, rows, buckets, width = r.activations.shape
     chips, units, head_width = r.ends.shape[0] // 2, r.all_act.shape[-1], r.all_mix.shape[-1]
-
-    @pl.when(step == 0)
-    def _():
-        sums = r.ends[0]
-        for other in range(1, 2 * chips):
-            sums = sums + r.ends[other]
-        singles = (r.ln1_gain, r.ln1_shift, r.ln2_gain, r.ln2_shift, r.b_out, r.b_proj)
-        for place, single in enumerate(singles):
-            single[...] = sums[place : place + 1]
-        for chip in range(chips):
-            both = r.ends[chip] + r.ends[chips + chip]
-            r.b_fc[:, chip * units : (chip + 1) * units] = both[6:7, :units]
-            here = slice(chip * head_width, (chip + 1) * head_width)
-            r.b_qv[0:1, here] = both[7:8, :head_width]
-            r.b_qv[1:2, here] = both[7:8, width // 2 : width // 2 + head_width]
-        for target, source in ((r.activations, r.acts), (r.in_grads, r.grads)):
-            for micro in range(micro_count):
-                rows_of = [
-                    source[micro * buckets + bucket].astype(F32)[:, None, :]
-                    for bucket in range(buckets)
-                ]
-                target[micro] = jnp.concatenate(rows_of, axis=1).astype(LOW)
-        for target in (r.w_qkv, r.w_out, r.w_fc, r.w_proj):
-            target[...] = jnp.zeros_like(target)
-
-    def rows_of_sequence(ref):
-        return ref[0].reshape(2 * chips * rows, ref.shape[-1])
-
-    nrm, nmlp, ups, brn, act, gpre, mix = (
-        rows_of_sequence(ref)
-        for ref in (r.all_nrm, r.all_nmlp, r.all_ups, r.all_brn, r.all_act, r.all_gpre, r.all_mix)
-    )
-    r.w_proj[...] += dot_tn(act, ups)
-    r.w_fc[...] += dot_tn(nmlp, gpre)
-    r.w_out[...] += dot_tn(mix, brn)
+    lines = r.acts.shape[0]
+    loads = [
+        pltpu.make_async_copy(source, target, r.load_sem.at[place])
+        for place, (source, target) in enumerate(
+            (
+                (r.all_act, r.act),
+                (r.all_ups, r.ups),
+                (r.all_nmlp, r.nmlp),
+                (r.all_gpre, r.gpre),
+                (r.all_mix, r.mix),
+                (r.all_brn, r.brn),
+                (r.all_nrm, r.nrm),
+                (r.all_dqkv, r.dqkv),
+            )
+        )
+    ]
+    stores = [
+        pltpu.make_async_copy(source, target, r.store_sem.at[place])
+        for place, (source, target) in enumerate(
+            (
+                (r.own_proj, r.w_proj),
+                (r.own_fc, r.w_fc),
+                (r.own_out, r.w_out),
+                (r.own_qkv, r.w_qkv),
+            )
+        )
+    ]
+    for load in loads:
+        load.start()
+
+    sums = r.ends[0]
+    for other in range(1, 2 * chips):
+        sums = sums + r.ends[other]
+    singles = (r.ln1_gain, r.ln1_shift, r.ln2_gain, r.ln2_shift, r.b_out, r.b_proj)
+    for place, single in enumerate(singles):
+        single[...] = sums[place : place + 1]
+    for chip in range(chips):
+        both = r.ends[chip] + r.ends[chips + chip]
+        r.b_fc[:, chip * units : (chip + 1) * units] = both[6:7, :units]
+        here = slice(chip * head_width, (chip + 1) * head_width)
+        r.b_qv[0:1, here] = both[7:8, :head_width]
+        r.b_qv[1:2, here] = both[7:8, width // 2 : width // 2 + head_width]
+    for target, source in ((r.activations, r.acts), (r.in_grads, r.grads)):
+        for micro in range(micro_count):
+            rows_of = [
+                source[micro * buckets + bucket].astype(F32)[:, None, :]
+                for bucket in range(buckets)
+            ]
+            target[micro] = jnp.concatenate(rows_of, axis=1).astype(LOW)
+
+    def flat(array):
+        return array.reshape(lines * 2 * chips * rows, array.shape[-1])
+
+    loads[0].wait()
+    loads[1].wait()
+    r.own_proj[...] = dot_tn(flat(r.act[...]), flat(r.ups[...]))
+    stores[0].start()
+    loads[2].wait()
+    loads[3].wait()
+    r.own_fc[...] = dot_tn(flat(r.nmlp[...]), flat(r.gpre[...]))
+    stores[1].start()
+    loads[4].wait()
+    loads[5].wait()
+    r.own_out[...] = dot_tn(flat(r.mix[...]), flat(r.brn[...]))
+    stores[2].start()
+    loads[6].wait()
+    loads[7].wait()
+    nrm = flat(r.nrm[...])
     for which in range(3):
-        grad = r.all_dqkv[0, :, which].reshape(2 * chips * rows, head_width)
-        r.w_qkv[which] += dot_tn(grad, nrm)
+        r.own_qkv[which] = dot_tn(flat(r.dqkv[:, :, which]), nrm)
+    stores[3].start()
+    for store in stores:
+        store.wait()
 
 
 def weights_call(relayed, inputs_shape, head_width, units):
-    lines = lax.axis_size("section")
     chips = lax.axis_size("tensor")
     width = inputs_shape[-1]
     half = width // 2
@@ -1584,23 +1697,20 @@
         w_proj=((units, half), F32),
         b_proj=((1, width), F32),
     )
-
-    def spec(array):
-        if len(array.shape) < 5:
-            return pl.BlockSpec(array.shape, lambda step: (0,) * len(array.shape))
-        return pl.BlockSpec(
-            (1,) + array.shape[1:], lambda step: (step,) + (0,) * (len(array.shape) - 1)
-        )
-
-    def whole(shape):
-        return pl.BlockSpec(shape, lambda step: (0,) * len(shape))
-
+    rows = ("act", "ups", "nmlp", "gpre", "mix", "brn", "nrm", "dqkv")
+    own = dict(own_proj="w_proj", own_fc="w_fc", own_out="w_out", own_qkv="w_qkv")
+    scratch = {name: pltpu.VMEM(relayed["all_" + name].shape, LOW) for name in rows}
+    scratch.update({name: pltpu.VMEM(outputs[of][0], F32) for name, of in own.items()})
+    scratch["load_sem"] = pltpu.SemaphoreType.DMA((8,))
+    scratch["store_sem"] = pltpu.SemaphoreType.DMA((4,))
+    whole, apart = pl.BlockSpec(memory_space=pltpu.VMEM), pl.BlockSpec(memory_space=pl.ANY)
+    small = ("acts", "grads", "ends")
     return pl.pallas_call(
-        functools.partial(weights_kernel, tuple(relayed) + tuple(outputs)),
+        functools.partial(weights_kernel, tuple(relayed) + tuple(outputs) + tuple(scratch)),
         out_shape=[jax.ShapeDtypeStruct(shape, kind) for shape, kind in outputs.values()],
-        grid=(lines,),
-        in_specs=[spec(array) for array in relayed.values()],
-        out_specs=[whole(shape) for shape, _ in outputs.values()],
+        in_specs=[whole if name in small else apart for name in relayed],
+        out_specs=[apart if name in own.values() else whole for name in outputs],
+        scratch_shapes=list(scratch.values()),
         compiler_params=pltpu.CompilerParams(vmem_limit_bytes=60 * 2**20),
         name="weight_gradients",
     )(*relayed.values())

time: 258 us -> 255 us (0.988)
  Pallas kernels: 257 us -> 254 us
where the time goes in v1:
time: 255 us
  Pallas kernels  254 us (100%)
    pallas_call x1, Pallas kernels, relay_call(): pl.pallas_call(functools.partial(relay_kernel, names), out_shape=[jax.Sha...  246 us
    pallas_call x1, Pallas kernels, weights_call(): pl.pallas_call(functools.partial(weights_kernel, tuple(relayed) + tuple(o...  7.93 us

profile of v1, /device:TPU:1, one launch (start us, length us, event | category | flops | bytes accessed | tf_op | source)
XLA Modules:
  0.0 254.9 jit_solution(1263814811131092705)
XLA Ops:
  0.7 246.1 %relay.1 = (bf16[4,32,768]{2,1,0:T(8,128)(2,1)}, bf16[4,32,768]{2,1,0:T(8,128)(2,1)}, f32[8,8,768]{2,1,0:T(8,128)}, bf16[4,2,2,64,384]{4,3,2,1,0:T(8,128)(2,1)},...) custom-call(bf16[2,32,2,768]{3,2,1,0:T(2,128)(2,1)} %refs_0_.1, ...), custom_call_target="tpu_custom_call" | custom-call | tf_op jit(solution)/shard_map/relay/pallas_call | solution.py:1584
  246.8 7.9 %weight_gradients.1 = (bf16[2,32,2,768]{3,2,1,0:T(2,128)(2,1)}, bf16[2,32,2,768]{3,2,1,0:T(2,128)(2,1)}, f32[1,768]{1,0:T(1,128)}, f32[1,768]{1,0:T(1,128)}, f32...) custom-call(bf16[4,32,768]{2,1,0:T(8,128)(2,1)} %get-tuple-element.3, ...), custom_call_target="tpu_custom_call" | custom-call | tf_op jit(solution)/shard_map/weight_gradients/pallas_call | solution.py:1708

commit v2 on v1

--- a/solution.py
+++ b/solution.py
@@ -628,6 +628,18 @@
     mine = row_block(t - 1, owned)
     my_half = row_block(c, local)
 
+    def store(p):
+        return (r.wq, r.wo, r.wf, r.wp)[p]
+
+    def source(p):
+        return (r.wq_in, r.wo_in, r.wf_in, r.wp_in)[p]
+
+    def own_copy(p):
+        return pltpu.make_async_copy(source(p), store(p).at[a], r.w_own.at[p])
+
+    for p in range(4):
+        own_copy(p).start()
+
     r.kv[...] = jnp.zeros(r.kv.shape, LOW)
 
     barrier = pltpu.get_barrier_semaphore()
@@ -651,12 +663,6 @@
     def above(s):
         return (s + 2) % 4
 
-    def store(p):
-        return (r.wq, r.wo, r.wf, r.wp)[p]
-
-    def source(p):
-        return (r.wq_in, r.wo_in, r.wf_in, r.wp_in)[p]
-
     def height(p):
         return source(p).shape[0]
 
@@ -665,7 +671,7 @@
 
     def first_hop(p, s, neighbour, which):
         return remote(
-            source(p).at[row_block(c, height(p) // 2)],
+            core_half(p, s, c),
             core_half(p, s, c),
             r.w_first_s.at[p, which],
             r.w_first_r.at[s, p],
@@ -682,9 +688,6 @@
         view = core_half(p, s, core)
         return remote(view, view, r.w_core_s.at[s, p], r.w_core_r.at[s, p], seq=1 - c)
 
-    def own_copy(p):
-        return pltpu.make_async_copy(source(p), store(p).at[a], r.w_own.at[p])
-
     def pass_on(s, p, which):
         line = (beside(s), above(s))[which]
 
@@ -712,10 +715,6 @@
             if p < 2:
                 pass_all(0, (p,))
             pass_far(0, p)
-
-        @pl.when(a == s)
-        def _():
-            own_copy(p).wait()
 
         @pl.when(a != s)
         def _():
@@ -744,10 +743,9 @@
     for step in range(1, lines):
         small_copy(step - 1, (a + step) % lines, a).start()
     for p in range(4):
+        own_copy(p).wait()
         for which, line in enumerate((beside(a), above(a))):
             first_hop(p, a, line, which).start()
-    for p in range(4):
-        own_copy(p).start()
     r.small[a] = r.small_own[...]
 
     def iota(shape, dimension):
@@ -1581,12 +1579,13 @@
         ends_r=dma,
     )
     names = tuple(operands) + tuple(outputs) + tuple(scratch)
+    apart = ("all_nrm", "all_nmlp", "all_ups", "all_brn")
     results = pl.pallas_call(
         functools.partial(relay_kernel, names),
         out_shape=[jax.ShapeDtypeStruct(shape, kind) for shape, kind in outputs.values()],
         in_specs=[pl.BlockSpec(memory_space=space(name)) for name in operands],
         out_specs=[
-            pl.BlockSpec(memory_space=pl.ANY if name in gathered else pltpu.VMEM)
+            pl.BlockSpec(memory_space=pl.ANY if name in apart else pltpu.VMEM)
             for name in outputs
         ],
         scratch_shapes=list(scratch.values()),

time: 255 us -> 256 us (level)
  no operation moved by 1% of the time
where the time goes in v2:
time: 256 us
  Pallas kernels  255 us (100%)
    pallas_call x1, Pallas kernels, relay_call(): pl.pallas_call(functools.partial(relay_kernel, names), out_shape=[jax.Sha...  247 us
    pallas_call x1, Pallas kernels, weights_call(): pl.pallas_call(functools.partial(weights_kernel, tuple(relayed) + tuple(o...  7.94 us

profile of v2, /device:TPU:1, one launch (start us, length us, event | category | flops | bytes accessed | tf_op | source)
XLA Modules:
  0.0 255.6 jit_solution(3067440989990779257)
XLA Ops:
  0.7 246.9 %relay.1 = (bf16[4,32,768]{2,1,0:T(8,128)(2,1)}, bf16[4,32,768]{2,1,0:T(8,128)(2,1)}, f32[8,8,768]{2,1,0:T(8,128)}, bf16[4,2,2,64,384]{4,3,2,1,0:T(8,128)(2,1)},...) custom-call(bf16[2,32,2,768]{3,2,1,0:T(2,128)(2,1)} %refs_0_.1, ...), custom_call_target="tpu_custom_call" | custom-call | tf_op jit(solution)/shard_map/relay/pallas_call | solution.py:1583
  247.5 7.9 %weight_gradients.1 = (bf16[2,32,2,768]{3,2,1,0:T(2,128)(2,1)}, bf16[2,32,2,768]{3,2,1,0:T(2,128)(2,1)}, f32[1,768]{1,0:T(1,128)}, f32[1,768]{1,0:T(1,128)}, f32...) custom-call(bf16[4,32,768]{2,1,0:T(8,128)(2,1)} %get-tuple-element.3, ...), custom_call_target="tpu_custom_call" | custom-call | tf_op jit(solution)/shard_map/weight_gradients/pallas_call | solution.py:1707

commit v3 on v1

--- a/solution.py
+++ b/solution.py
@@ -1150,12 +1150,18 @@
                     for other in streams:
                         kv_copy(s, other).wait_recv()
 
+            if j == STREAMS - 1:
+
+                @pl.when(s == 0)
+                def _():
+                    pass_all(0, (2,))
+
             attend_line(s, j)
             leave_attention(s, j)
 
         @pl.when(s == 0)
         def _():
-            pass_all(0, (2,))
+            pass_all(0, (3,))
             for later in range(1, lines):
                 pass_all(later, (0, 1, 2))
 
@@ -1171,7 +1177,7 @@
             between(s, j)
         @pl.when(s == 0)
         def _():
-            for later in range(lines):
+            for later in range(1, lines):
                 pass_all(later, (3,))
 
         need(s, 2)
@@ -1356,9 +1362,6 @@
     lax.fori_loop(0, lines, backward, 0)
 
     share(GPRE)
-    for line in range(lines):
-        drain(r.all_dqkv.at[line, c], r.heads_r.at[line])
-        share_heads(line, c).start()
 
     drain(r.norm_all, r.norm_r)
     slot = c * chips + t
@@ -1381,6 +1384,10 @@
 
     for step in range(1, 2 * chips):
         ends_copy(step).start()
+
+    for line in range(lines):
+        drain(r.all_dqkv.at[line, c], r.heads_r.at[line])
+        share_heads(line, c).start()
 
     for index in (UPS, GPRE):
 

time: 255 us -> 255 us (level)
  no operation moved by 1% of the time
where the time goes in v3:
time: 255 us
  Pallas kernels  254 us (100%)
    pallas_call x1, Pallas kernels, relay_call(): pl.pallas_call(functools.partial(relay_kernel, names), out_shape=[jax.Sha...  246 us
    pallas_call x1, Pallas kernels, weights_call(): pl.pallas_call(functools.partial(weights_kernel, tuple(relayed) + tuple(o...  7.93 us

profile of v3, /device:TPU:1, one launch (start us, length us, event | category | flops | bytes accessed | tf_op | source)
XLA Modules:
  0.0 254.9 jit_solution(6257372000293027775)
XLA Ops:
  0.7 246.1 %relay.1 = (bf16[4,32,768]{2,1,0:T(8,128)(2,1)}, bf16[4,32,768]{2,1,0:T(8,128)(2,1)}, f32[8,8,768]{2,1,0:T(8,128)}, bf16[4,2,2,64,384]{4,3,2,1,0:T(8,128)(2,1)},...) custom-call(bf16[2,32,2,768]{3,2,1,0:T(2,128)(2,1)} %refs_0_.1, ...), custom_call_target="tpu_custom_call" | custom-call | tf_op jit(solution)/shard_map/relay/pallas_call | solution.py:1591
  246.8 7.9 %weight_gradients.1 = (bf16[2,32,2,768]{3,2,1,0:T(2,128)(2,1)}, bf16[2,32,2,768]{3,2,1,0:T(2,128)(2,1)}, f32[1,768]{1,0:T(1,128)}, f32[1,768]{1,0:T(1,128)}, f32...) custom-call(bf16[4,32,768]{2,1,0:T(8,128)(2,1)} %get-tuple-element.3, ...), custom_call_target="tpu_custom_call" | custom-call | tf_op jit(solution)/shard_map/weight_gradients/pallas_call | solution.py:1715
